TPU v7x, 32 devices: a whole 2x2x4 slice. The times are simulated.
32 devices in a mesh: slides: 2 (over x), seq: 16 (over z, y, core).
Axes of the slice: x: 2, y: 2, z: 4, core: 2. Of those that a mesh axis runs over, the one named last changes fastest.
Arguments:
- tiles: bfloat16 [16384, 768], P(('slides', 'seq')), parts along dimension 0, may hold values from -6 to 6
- tile_count: int32 [2], P('slides'), parts along dimension 0, may hold values from 4096 to 8192
- conv_weight: float32 [25, 768], replicated, may hold values from -3 to 3
- conv_bias: float32 [768], replicated, may hold values from -3 to 3
- ln_gain: float32 [768], replicated, may hold values from 0.1 to 1.9
- w_qkv: bfloat16 [768, 2304], replicated, may hold values from -5 to 5
- w_out: bfloat16 [768, 768], replicated, may hold values from -0.21875 to 0.21875
Outputs:
- attended: bfloat16 [16384, 768], P(('slides', 'seq')), parts along dimension 0
- encoded: bfloat16 [16384, 768], P(('slides', 'seq')), parts along dimension 0
There are 2 independent parts, one for each index of `slides`. A program takes and returns all parts, laid end to end along the dimension named above; an argument that names none is the same for every part. Nothing has to cross between parts.
All inputs are finite; a program needn't handle non-finite values.
Results may differ from a plain program's by a relative error of at most 0.0051.
Values may be sent and summed in bfloat16 or wider, within the bound.
A program may use at most 128 MiB of HBM per device.

v0:
```python
import jax
import jax.numpy as jnp
from jax import lax
from jax.sharding import PartitionSpec as P

ATTENTION_HEADS = 16
GW = 128
MID_RATE = 8


EPS = 1e-05
NEG = -1e30


def extended(block, sides, width):
    for axis, dim in sides:
        count = lax.axis_size(axis)
        forward = [(i, i + 1) for i in range(count - 1)]
        backward = [(target, source) for source, target in forward]
        low = lax.ppermute(
            lax.slice_in_dim(block, block.shape[dim] - width, None, axis=dim), axis, forward
        )
        high = lax.ppermute(lax.slice_in_dim(block, 0, width, axis=dim), axis, backward)
        block = jnp.concatenate([low, block, high], axis=dim)
    return block


def permitted_mask(query_index, key_index, dilation_step, active_count, head_total):
    shift_amounts = jnp.arange(head_total, dtype=jnp.int32) % dilation_step
    key_position = shift_amounts[:, None] + dilation_step * key_index[None, :]
    key_live = key_position < active_count
    return key_live[:, None, :] | (query_index[None, :, None] == key_index[None, None, :])


def attend_single_block(query_portion, key_portion, value_portion, allowed):
    score_scale = query_portion.shape[2] ** (-0.5)
    scores = (
        jnp.einsum("qhd,khd->hqk", query_portion, key_portion, preferred_element_type=jnp.float32)
        * score_scale
    )
    scores = jnp.where(allowed, scores, NEG)
    row_top = jnp.max(scores, axis=2, keepdims=True)
    exp_terms = jnp.where(allowed, jnp.exp(scores - row_top), 0.0)
    denom_sum = jnp.sum(exp_terms, axis=2)
    weights = exp_terms.astype(jnp.bfloat16)
    summed = jnp.einsum("hqk,khd->qhd", weights, value_portion, preferred_element_type=jnp.float32)
    level_lse = jnp.transpose(row_top[:, :, 0] + jnp.log(denom_sum))
    return (summed / jnp.transpose(denom_sum)[:, :, None], level_lse)


def offset_keep(dilation_step, model_width, head_size):
    step_index = jnp.arange(dilation_step, dtype=jnp.int32)[:, None]
    column_head = jnp.arange(model_width, dtype=jnp.int32)[None, :] // head_size
    return step_index == column_head % dilation_step


def dilated_rows(source_rows, dilation_step, head_size):
    model_width = source_rows.shape[1]
    grouped_rows = source_rows.reshape(
        source_rows.shape[0] // dilation_step, dilation_step, model_width
    )
    keep = offset_keep(dilation_step, model_width, head_size)
    return jnp.sum(jnp.where(keep[None], grouped_rows, jnp.zeros((), source_rows.dtype)), axis=1)


def scatter_back(sparse_output, sparse_logsumexp, dilation_step, head_size):
    sparse_rows, heads_total = sparse_logsumexp.shape
    model_width = heads_total * head_size
    flat_out = sparse_output.reshape(sparse_rows, model_width)
    keep = offset_keep(dilation_step, model_width, head_size)
    widened = jnp.where(keep[None], flat_out[:, None, :], 0.0)
    match_flag = (
        jnp.arange(dilation_step)[:, None] == (jnp.arange(heads_total) % dilation_step)[None, :]
    )
    lse_wide = jnp.where(match_flag[None], sparse_logsumexp[:, None, :], NEG)
    output_rows = sparse_rows * dilation_step
    return (
        widened.reshape(output_rows, heads_total, head_size),
        lse_wide.reshape(output_rows, heads_total),
    )


def merge_levels(level_outs, level_lses):
    top_all = jnp.maximum(jnp.maximum(level_lses[0], level_lses[1]), level_lses[2])
    factors = [jnp.exp(one_lse - top_all) for one_lse in level_lses]
    numer = (
        factors[0][:, :, None] * level_outs[0]
        + factors[1][:, :, None] * level_outs[1]
        + factors[2][:, :, None] * level_outs[2]
    )
    return numer / (factors[0] + factors[1] + factors[2])[:, :, None]


def positional_sum(padded, column, conv_weight, halo_width, out_rows):
    summed = jnp.zeros((out_rows, padded.shape[1]), jnp.float32)
    for row_step in range(-2, 3):
        for col_step in range(-2, 3):
            start_row = halo_width + row_step * GW + col_step
            window = padded[start_row : start_row + out_rows].astype(jnp.float32)
            inside = ((column + col_step >= 0) & (column + col_step < GW)).astype(jnp.float32)
            summed = summed + window * (
                conv_weight[(row_step + 2) * 5 + col_step + 2][None, :] * inside[:, None]
            )
    return summed


def normalize(mixed_in, ln_gain):
    row_mean = jnp.mean(mixed_in, axis=1, keepdims=True)
    centred = mixed_in - row_mean
    row_var = jnp.mean(centred * centred, axis=1, keepdims=True)
    return (centred * lax.rsqrt(row_var + EPS) * ln_gain).astype(jnp.bfloat16)


def shards(tiles, tile_count, conv_weight, conv_bias, ln_gain, w_qkv, w_out):
    local_rows = tiles.shape[0]
    model_width = tiles.shape[1]
    head_size = model_width // ATTENTION_HEADS
    devices = lax.axis_size("seq")
    dev_index = lax.axis_index("seq")
    active_count = tile_count[0]
    position = dev_index * local_rows + jnp.arange(local_rows, dtype=jnp.int32)
    valid_row = (position < active_count).astype(jnp.float32)[:, None]
    masked = tiles * valid_row.astype(jnp.bfloat16)
    halo_width = 2 * GW + 2
    padded = extended(masked, (("seq", 0),), halo_width)
    column = jnp.arange(local_rows, dtype=jnp.int32) % GW
    summed = positional_sum(padded, column, conv_weight, halo_width, local_rows)
    mixed_in = (masked.astype(jnp.float32) + summed + conv_bias) * valid_row
    normed = normalize(mixed_in, ln_gain)
    projected = jnp.dot(normed, w_qkv, preferred_element_type=jnp.float32).astype(jnp.bfloat16)
    query_flat = projected[:, :model_width]
    key_flat = projected[:, model_width : 2 * model_width]
    value_flat = projected[:, 2 * model_width :]

    def heads_of(flat_rows):
        return flat_rows.reshape(flat_rows.shape[0], ATTENTION_HEADS, head_size)

    near_out, near_lse = attend_single_block(
        heads_of(query_flat),
        heads_of(key_flat),
        heads_of(value_flat),
        permitted_mask(position, position, 1, active_count, ATTENTION_HEADS),
    )
    mid_rows = local_rows // MID_RATE
    mid_query = heads_of(dilated_rows(query_flat, MID_RATE, head_size))
    mid_kv = jnp.stack(
        [dilated_rows(key_flat, MID_RATE, head_size), dilated_rows(value_flat, MID_RATE, head_size)]
    )
    mid_query_idx = dev_index * mid_rows + jnp.arange(mid_rows, dtype=jnp.int32)
    group_base = dev_index // MID_RATE * local_rows
    far_rows = local_rows // devices
    far_query = heads_of(dilated_rows(query_flat, devices, head_size))
    far_kv = jnp.stack(
        [dilated_rows(key_flat, devices, head_size), dilated_rows(value_flat, devices, head_size)]
    )
    far_query_idx = dev_index * far_rows + jnp.arange(far_rows, dtype=jnp.int32)
    mid_all, far_all = (
        lax.all_gather(mid_kv, "seq", axis=1, tiled=True),
        lax.all_gather(far_kv, "seq", axis=1, tiled=True),
    )
    group_kv = lax.dynamic_slice_in_dim(mid_all, group_base, local_rows, 1)
    far_keys_idx = jnp.arange(local_rows, dtype=jnp.int32)
    far_sparse, far_sparse_lse = attend_single_block(
        far_query,
        heads_of(far_all[0]),
        heads_of(far_all[1]),
        permitted_mask(far_query_idx, far_keys_idx, devices, active_count, ATTENTION_HEADS),
    )
    group_idx = group_base + jnp.arange(local_rows, dtype=jnp.int32)
    mid_sparse, mid_sparse_lse = attend_single_block(
        mid_query,
        heads_of(group_kv[0]),
        heads_of(group_kv[1]),
        permitted_mask(mid_query_idx, group_idx, MID_RATE, active_count, ATTENTION_HEADS),
    )
    mid_out, mid_lse = scatter_back(mid_sparse, mid_sparse_lse, MID_RATE, head_size)
    far_out, far_lse = scatter_back(far_sparse, far_sparse_lse, devices, head_size)
    heads_all = merge_levels((near_out, mid_out, far_out), (near_lse, mid_lse, far_lse))
    attended = (heads_all.reshape(local_rows, model_width) * valid_row).astype(jnp.bfloat16)
    encoded = (
        (mixed_in + jnp.dot(attended, w_out, preferred_element_type=jnp.float32)) * valid_row
    ).astype(jnp.bfloat16)
    return (attended, encoded)


def solution(mesh):
    placed = (P(("slides", "seq"), None), P("slides"), P(), P(), P(), P(), P())
    return jax.shard_map(
        shards,
        mesh=mesh,
        in_specs=placed,
        out_specs=(P(("slides", "seq"), None), P(("slides", "seq"), None)),
        check_vma=False,
    )
```

profile of v0, /device:TPU:0, one launch (start us, length us, event | category | flops | bytes accessed | tf_op | source)
XLA Modules:
  0.0 183.0 jit_solution(1952805897172357728)
XLA Ops:
  8.1 0.5 copy-done.30
  8.6 1.3 broadcast_multiply_fusion
  10.0 1.3 collective-permute-start.1
  11.3 3.1 %collective-permute-start = (bf16[258,768]{1,0:T(8,128)(2,1)S(1)}, bf16[258,768]{1,0:T(8,128)(2,1)S(1)}, u32[]{:S(2)}, u32[]{:S(2)}) collective-permute-start(bf16[258,768]{1,0:T(8,128)(2,1)S(1)} %get-tuple-element.48), channel_id=1, source_target_pairs={{0,1},{1,2},{2,3},{3,4},{4,5},{5,6},{6,7},{7,8},{8,9},{9,10},{10,1... | collective-permute-start | bytes 1188872 | tf_op jit(solution)/shard_map/ppermute | solution.py:20
  14.7 1.0 collective-permute-done
  15.7 20.1 %fusion.97 = (f32[512]{0:T(512)S(1)}, f32[512,768]{1,0:T(8,128)S(1)}) fusion(f32[512]{0:T(512)S(1)} %get-tuple-element.39, f32[768]{0:T(1024)S(1)} %copy-done.29, f32[768]{0:T(1024)S(1)} %get-tuple-element.31, bf16[258,768]{1,0:T(8,128)(2,1)S(1)} %collective-permute-done.1, bf16[512,768]{1,0:T(8,128)(2,1)S(1)} %broadcast_multiply_fusion, ...), kind=kLoop, calls=%fused_computation.238 | loop fusion | flops 68812288 | bytes 3246080 | tf_op jit(solution)/shard_map/reduce_sum | solution.py:108
  35.8 0.3 multiply_reduce_fusion
  36.1 0.4 copy-done.34
  36.5 2.1 %convolution_convert_fusion = bf16[512,2304]{1,0:T(8,128)(2,1)S(1)} fusion(bf16[768,2304]{1,0:T(8,128)(2,1)S(1)} %copy-done, f32[512,768]{1,0:T(8,128)S(1)} %get-tuple-element.38, f32[768]{0:T(1024)S(1)} %copy-done.34, f32[512]{0:T(512)S(1)} %add_rsqrt_fusion, f32[512]{0:T(512)S(1)} %broadcast_multiply_fusion.2), kind=kOutput, calls=%fused_computation.8 | convolution fusion | flops 1814691840 | bytes 7478272 | tf_op jit(solution)/shard_map/dot_general | solution.py:130
  38.6 1.4 copy-done.2
  40.0 0.7 select_reduce_fusion.2
  40.8 0.7 copy.63
  42.0 2.9 %fusion.66 = (bf16[64,768]{1,0:T(8,128)(2,1)S(1)}, bf16[64,768]{1,0:T(8,128)(2,1)S(1)}, bf16[64,768]{1,0:T(8,128)(2,1)S(1)}) fusion(pred[8,768]{1,0:T(8,128)(4,1)S(1)} %iota_compare_fusion.2, bf16[512,2304]{1,0:T(8,128)(2,1)} %copy-done.2), kind=kLoop, calls=%fused_computation.127 | loop fusion | flops 2211840 | bytes 2660352 | tf_op jit(solution)/shard_map/reduce_sum | solution.py:63
  44.9 0.9 copy.58
  45.8 0.6 iota_compare_fusion.4
  46.4 0.7 iota_compare_fusion.3
  47.2 0.7 add_compare_fusion
  47.8 0.7 broadcast_compare_fusion.1
  48.9 0.8 copy.77
  49.7 1.3 fusion.100
  51.0 2.4 %copy.66 = bf16[512,768]{0,1:T(8,128)(2,1)} copy(bf16[512,768]{1,0:T(8,128)(2,1)} %get-tuple-element.44) | data formatting | bytes 1572864 | tf_op jit(solution)/shard_map/slice | solution.py:133
  53.7 0.3 copy.57
  54.0 4.4 %fusion = (f32[16,512]{1,0:T(8,128)S(1)}, f32[16,512,512]{1,2,0:T(8,128)S(1)}) fusion(pred[512,512]{0,1:T(8,128)(4,1)S(1)} %broadcast_compare_fusion, pred[512]{0:T(512)(128)(4,1)S(1)} %copy-done.31, bf16[512,16,48]{0,2,1:T(8,128)(2,1)S(1)} %bitcast.108, bf16[512,16,48]{0,2,1:T(8,128)(2,1)S(1)} %bitcast.109), kind=kOutput, calls=%fused_computation.2 | convolution fusion | flops 419422208 | bytes 18645504 | tf_op jit(solution)/shard_map/qhd,khd->hqk/dot_general | solution.py:38
  58.4 5.7 %copy-done.4 = f32[16,512,512]{1,2,0:T(8,128)} copy-done((f32[16,512,512]{1,2,0:T(8,128)}, f32[16,512,512]{1,2,0:T(8,128)S(1)}, u32[]{:S(2)}) %copy-start.4) | copy-done | bytes 16777240
  64.1 5.1 %fusion.2 = f32[16,512]{1,0:T(8,128)} fusion(f32[16,512,512]{1,2,0:T(8,128)S(1)} %get-tuple-element.55, f32[16,512]{1,0:T(8,128)S(1)} %get-tuple-element.54, pred[512,512]{0,1:T(8,128)(4,1)S(1)} %broadcast_compare_fusion, pred[512]{0:T(512)(128)(4,1)S(1)} %copy-done.31), kind=kLoop, calls=%fused_computation.4 | loop fusion | flops 25157632 | bytes 17105408 | tf_op jit(solution)/shard_map/reduce_sum | solution.py:44
  69.2 22.7 %all-gather.5.cloned.1.call-done = bf16[2,512,768]{2,0,1:T(2,128)(2,1)} async-done(((bf16[2,32,768]{2,0,1:T(2,128)(2,1)}), bf16[2,512,768]{2,0,1:T(2,128)(2,1)}) %all-gather.5.cloned.1.call-update) | async-done | bytes 1572880 | tf_op jit(solution)/shard_map/all_gather | solution.py:159
  91.9 4.3 %fusion.101 = (bf16[1,512,768]{2,0,1:T(2,128)(2,1)S(1)}, bf16[1,512,768]{2,0,1:T(2,128)(2,1)S(1)}) fusion(bf16[2,512,768]{2,0,1:T(2,128)(2,1)} %all-gather.5.cloned.1.call-done), kind=kLoop, calls=%fused_computation.241 | loop fusion | bytes 3145728 | tf_op jit(solution)/shard_map/slice | solution.py:165
  96.2 3.3 %copy.72 = bf16[1,512,768]{1,2,0:T(8,128)(2,1)} copy(bf16[1,512,768]{2,0,1:T(2,128)(2,1)S(1)} %get-tuple-element.47) | data formatting | bytes 1572864 | tf_op jit(solution)/shard_map/slice | solution.py:166
  99.5 2.0 %copy.64 = bf16[1,512,768]{1,2,0:T(8,128)(2,1)S(1)} copy(bf16[1,512,768]{2,0,1:T(2,128)(2,1)S(1)} %get-tuple-element.46) | data formatting | bytes 1572864 | tf_op jit(solution)/shard_map/slice | solution.py:165
  101.4 1.2 fusion.103
  102.6 0.4 fusion.41
  103.1 0.4 fusion.33
  104.0 3.4 %select_n.297 = f32[512,16,48]{2,1,0:T(8,128)} reshape(f32[32,16,768]{2,1,0:T(8,128)S(1)} %broadcast_select_fusion) | data formatting | bytes 3145728 | tf_op jit(solution)/shard_map/jit(_where)/select_n | solution.py:71
  107.4 3.7 %copy.74 = f32[512,16,48]{0,2,1:T(8,128)} copy(f32[512,16,48]{2,1,0:T(8,128)} %select_n.297) | data formatting | bytes 3145728 | tf_op jit(solution)/shard_map/jit(_where)/select_n | solution.py:71
  111.4 26.9 %all-gather.3.cloned.1.call-done = bf16[2,1024,768]{2,0,1:T(2,128)(2,1)} async-done(((bf16[2,64,768]{2,0,1:T(2,128)(2,1)}), bf16[2,1024,768]{2,0,1:T(2,128)(2,1)}) %all-gather.3.cloned.1.call-update) | async-done | bytes 3145744 | tf_op jit(solution)/shard_map/all_gather | solution.py:158
  138.3 4.4 %constant_dynamic-slice_fusion = (bf16[1,512,768]{2,0,1:T(2,128)(2,1)S(1)}, bf16[1,512,768]{2,0,1:T(2,128)(2,1)S(1)}) fusion(bf16[2,1024,768]{2,0,1:T(2,128)(2,1)} %all-gather.3.cloned.1.call-done, s32[]{:T(128)S(6)} %select_n.280, s32[]{:T(128)S(6)} %add.568), kind=kLoop, calls=%fused_computation.229 | loop fusion | bytes 3145736 | tf_op jit(solution)/shard_map/slice | solution.py:172
  142.7 3.3 %copy.69 = bf16[1,512,768]{1,2,0:T(8,128)(2,1)} copy(bf16[1,512,768]{2,0,1:T(2,128)(2,1)S(1)} %get-tuple-element.42) | data formatting | bytes 1572864 | tf_op jit(solution)/shard_map/slice | solution.py:173
  146.0 2.2 %copy.59 = bf16[1,512,768]{1,2,0:T(8,128)(2,1)S(1)} copy(bf16[1,512,768]{2,0,1:T(2,128)(2,1)S(1)} %get-tuple-element.41) | data formatting | bytes 1572864 | tf_op jit(solution)/shard_map/slice | solution.py:172
  148.2 0.7 fusion.7
  148.9 0.9 fusion.31
  150.1 1.7 fusion.32
  151.8 1.1 copy.70
  153.1 3.4 %select_n.295 = f32[512,16,48]{2,1,0:T(8,128)} reshape(f32[64,8,768]{2,1,0:T(8,128)S(1)} %broadcast_select_fusion.1) | data formatting | bytes 3145728 | tf_op jit(solution)/shard_map/jit(_where)/select_n | solution.py:71
  156.5 3.8 %copy.71 = f32[512,16,48]{0,2,1:T(8,128)} copy(f32[512,16,48]{2,1,0:T(8,128)} %select_n.295) | data formatting | bytes 3145728 | tf_op jit(solution)/shard_map/jit(_where)/select_n | solution.py:71
  160.6 8.7 %fusion.26 = f32[512,16,48]{0,2,1:T(8,128)S(1)} fusion(f32[512,16,48]{0,2,1:T(8,128)S(1)} %copy-done.8, f32[512,16,48]{0,2,1:T(8,128)} %copy.71, bf16[512,16,48]{0,2,1:T(8,128)(2,1)} %bitcast.107, f32[16,512,512]{1,2,0:T(8,128)} %copy-done.4, f32[16,512]{1,0:T(8,128)S(1)} %copy-done.15, pred[512,512]{0,1:T(8,128)(4,1)S(1)} %broadcast_compare_fusion, ...), kind=kOutput, calls=%fused_computation.77 | convolution fusion | flops 430571520 | bytes 22741504 | tf_op jit(solution)/shard_map/hqk,khd->qhd/dot_general | solution.py:46
  169.3 1.6 copy.75
  171.0 1.7 multiply_convert_fusion.1
  172.8 3.3 %multiply_convert_fusion = bf16[512,768]{1,0:T(8,128)(2,1)} fusion(f32[512,768]{1,0:T(8,128)S(1)} %copy-done.6, bf16[512,768]{1,0:T(8,128)(2,1)S(1)} %multiply_convert_fusion.1, bf16[768,768]{1,0:T(8,128)(2,1)} %param.13, f32[512]{0:T(512)S(1)} %copy-done.27), kind=kOutput, calls=%fused_computation.78 | convolution fusion | flops 605159424 | bytes 4327424 | tf_op jit(solution)/shard_map/dot_general | solution.py:181
  (111 shorter events, 3.2 us)
Async XLA Ops:
  7.2 29.0 %copy-start = (bf16[768,2304]{1,0:T(8,128)(2,1)S(1)}, bf16[768,2304]{1,0:T(8,128)(2,1)}, u32[]{:S(2)}) copy-start(bf16[768,2304]{1,0:T(8,128)(2,1)} %param.12) | copy-start | bytes 10616836
  7.2 84.7 %all-gather.5.cloned.1.call-start = ((), (), s32[]{:S(2)}) async-start(), calls=%async_computation.1 | async-start | bytes 1671168 | tf_op jit(solution)/shard_map/all_gather | solution.py:159
  8.0 0.5 copy-start.30
  8.0 7.6 %copy-start.26 = (f32[512]{0:T(512)}, f32[512]{0:T(512)S(1)}, u32[]{:S(2)}) copy-start(f32[512]{0:T(512)S(1)} %get-tuple-element.39) | copy-start | bytes 6148
  8.6 5.8 %copy-start.23 = (f32[25,768]{1,0:T(8,128)S(1)}, f32[25,768]{1,0:T(8,128)}, u32[]{:S(2)}) copy-start(f32[25,768]{1,0:T(8,128)} %param.9) | copy-start | bytes 230404
  8.6 7.1 %copy-start.29 = (f32[768]{0:T(1024)S(1)}, f32[768]{0:T(1024)}, u32[]{:S(2)}) copy-start(f32[768]{0:T(1024)} %param.10) | copy-start | bytes 9220
  10.0 4.7 %collective-permute-start.1 = (bf16[258,768]{1,0:T(8,128)(2,1)S(1)}, bf16[258,768]{1,0:T(8,128)(2,1)S(1)}, u32[]{:S(2)}, u32[]{:S(2)}) collective-permute-start(bf16[258,768]{1,0:T(8,128)(2,1)S(1)} %get-tuple-element.49), channel_id=1, source_target_pairs={{1,0},{2,1},{3,2},{4,3},{5,4},{6,5},{7,6},{8,7},{9,8},{10,9},{11,1... | collective-permute-start | bytes 1188872 | tf_op jit(solution)/shard_map/ppermute | solution.py:23
  11.3 4.4 %collective-permute-start = (bf16[258,768]{1,0:T(8,128)(2,1)S(1)}, bf16[258,768]{1,0:T(8,128)(2,1)S(1)}, u32[]{:S(2)}, u32[]{:S(2)}) collective-permute-start(bf16[258,768]{1,0:T(8,128)(2,1)S(1)} %get-tuple-element.48), channel_id=1, source_target_pairs={{0,1},{1,2},{2,3},{3,4},{4,5},{5,6},{6,7},{7,8},{8,9},{9,10},{10,1... | collective-permute-start | bytes 1188872 | tf_op jit(solution)/shard_map/ppermute | solution.py:20
  14.7 24.0 %copy-start.17 = (pred[16,768]{1,0:T(8,128)(4,1)}, pred[16,768]{1,0:T(8,128)(4,1)S(1)}, u32[]{:S(2)}) copy-start(pred[16,768]{1,0:T(8,128)(4,1)S(1)} %iota_compare_fusion.1) | copy-start | bytes 36868
  35.8 2.8 %copy-start.5 = (f32[512,768]{1,0:T(8,128)}, f32[512,768]{1,0:T(8,128)S(1)}, u32[]{:S(2)}) copy-start(f32[512,768]{1,0:T(8,128)S(1)} %get-tuple-element.38) | copy-start | bytes 4718596
  35.8 0.7 copy-start.34
  38.6 1.4 copy-start.2
  41.6 96.7 %all-gather.3.cloned.1.call-start = ((), (), s32[]{:S(2)}) async-start(), calls=%async_computation | async-start | bytes 3342336 | tf_op jit(solution)/shard_map/all_gather | solution.py:158
  41.9 2.9 %copy-start.24 = (pred[8,768]{1,0:T(8,128)(4,1)}, pred[8,768]{1,0:T(8,128)(4,1)S(1)}, u32[]{:S(2)}) copy-start(pred[8,768]{1,0:T(8,128)(4,1)S(1)} %iota_compare_fusion.2) | copy-start | bytes 18436
  42.0 7.8 %copy-start.3 = (bf16[512,2304]{1,0:T(8,128)(2,1)S(1)}, bf16[512,2304]{1,0:T(8,128)(2,1)}, u32[]{:S(2)}) copy-start(bf16[512,2304]{1,0:T(8,128)(2,1)} %copy-done.2) | copy-start | bytes 7077892
  51.0 2.4 %copy-start.7 = (bf16[512,768]{1,0:T(8,128)(2,1)S(1)}, bf16[512,768]{1,0:T(8,128)(2,1)}, u32[]{:S(2)}) copy-start(bf16[512,768]{1,0:T(8,128)(2,1)} %get-tuple-element.45) | copy-start | bytes 2359300
  53.4 0.6 copy-start.31
  58.4 5.7 %copy-start.4 = (f32[16,512,512]{1,2,0:T(8,128)}, f32[16,512,512]{1,2,0:T(8,128)S(1)}, u32[]{:S(2)}) copy-start(f32[16,512,512]{1,2,0:T(8,128)S(1)} %get-tuple-element.55) | copy-start | bytes 50331652
  58.4 10.8 %copy-start.14 = (f32[16,512]{1,0:T(8,128)}, f32[16,512]{1,0:T(8,128)S(1)}, u32[]{:S(2)}) copy-start(f32[16,512]{1,0:T(8,128)S(1)} %get-tuple-element.54) | copy-start | bytes 98308
  101.4 1.2 copy-start.22
  101.4 1.6 copy-start.11
  102.6 0.9 copy-start.19
  103.0 0.7 copy-start.18
  107.4 3.7 %copy-start.20 = (f32[16,32]{1,0:T(8,128)S(1)}, f32[16,32]{1,0:T(8,128)}, u32[]{:S(2)}) copy-start(f32[16,32]{1,0:T(8,128)} %copy-done.19) | copy-start | bytes 6148
  107.4 3.7 %copy-start.28 = (pred[16,16]{0,1:T(8,128)(4,1)S(1)}, pred[16,16]{0,1:T(8,128)(4,1)}, u32[]{:S(2)}) copy-start(pred[16,16]{0,1:T(8,128)(4,1)} %iota_compare_fusion.3) | copy-start | bytes 772
  146.0 2.2 %copy-start.9 = (bf16[64,768]{0,1:T(8,128)(2,1)S(1)}, bf16[64,768]{0,1:T(8,128)(2,1)}, u32[]{:S(2)}) copy-start(bf16[64,768]{0,1:T(8,128)(2,1)} %copy.77) | copy-start | bytes 294916
  146.0 2.2 %copy-start.13 = (pred[64,512]{1,0:T(8,128)(4,1)S(1)}, pred[64,512]{1,0:T(8,128)(4,1)}, u32[]{:S(2)}) copy-start(pred[64,512]{1,0:T(8,128)(4,1)} %broadcast_compare_fusion.1) | copy-start | bytes 98308
  146.0 2.2 %copy-start.21 = (pred[16,512]{1,0:T(8,128)(4,1)S(1)}, pred[16,512]{1,0:T(8,128)(4,1)}, u32[]{:S(2)}) copy-start(pred[16,512]{1,0:T(8,128)(4,1)} %get-tuple-element.57) | copy-start | bytes 24580
  148.9 1.1 copy-start.10
  150.1 2.8 %copy-start.25 = (pred[8,768]{1,0:T(8,128)(4,1)S(1)}, pred[8,768]{1,0:T(8,128)(4,1)}, u32[]{:S(2)}) copy-start(pred[8,768]{1,0:T(8,128)(4,1)} %copy-done.24) | copy-start | bytes 18436
  156.5 4.0 %copy-start.33 = (pred[8,16]{1,0:T(8,128)(4,1)S(1)}, pred[8,16]{1,0:T(8,128)(4,1)}, u32[]{:S(2)}) copy-start(pred[8,16]{1,0:T(8,128)(4,1)} %iota_compare_fusion.4) | copy-start | bytes 388
  156.5 4.1 %copy-start.15 = (f32[16,512]{1,0:T(8,128)S(1)}, f32[16,512]{1,0:T(8,128)}, u32[]{:S(2)}) copy-start(f32[16,512]{1,0:T(8,128)} %copy-done.14) | copy-start | bytes 98308
  156.5 4.1 %copy-start.16 = (f32[16,512]{1,0:T(8,128)S(1)}, f32[16,512]{1,0:T(8,128)}, u32[]{:S(2)}) copy-start(f32[16,512]{1,0:T(8,128)} %fusion.2) | copy-start | bytes 98308
  156.5 4.1 %copy-start.8 = (f32[512,16,48]{0,2,1:T(8,128)S(1)}, f32[512,16,48]{0,2,1:T(8,128)}, u32[]{:S(2)}) copy-start(f32[512,16,48]{0,2,1:T(8,128)} %copy.74) | copy-start | bytes 4718596
  156.5 4.1 %copy-start.32 = (pred[512]{0:T(512)(128)(4,1)S(1)}, pred[512]{0:T(512)(128)(4,1)}, u32[]{:S(2)}) copy-start(pred[512]{0:T(512)(128)(4,1)} %copy-done.30) | copy-start | bytes 1540
  169.3 1.6 copy-start.27
  171.0 1.9 %copy-start.6 = (f32[512,768]{1,0:T(8,128)S(1)}, f32[512,768]{1,0:T(8,128)}, u32[]{:S(2)}) copy-start(f32[512,768]{1,0:T(8,128)} %copy-done.5) | copy-start | bytes 4718596
  171.0 5.2 %copy-start.1 = (bf16[768,2304]{1,0:T(8,128)(2,1)S(1)}, bf16[768,2304]{1,0:T(8,128)(2,1)}, u32[]{:S(2)}) copy-start(bf16[768,2304]{1,0:T(8,128)(2,1)} %param.12) | copy-start | bytes 10616836
  172.8 3.4 %copy-start.12 = (bf16[512,768]{1,0:T(8,128)(2,1)}, bf16[512,768]{1,0:T(8,128)(2,1)S(1)}, u32[]{:S(2)}) copy-start(bf16[512,768]{1,0:T(8,128)(2,1)S(1)} %multiply_convert_fusion.1) | copy-start | bytes 2359300
Sparse Core Ops, SparseCore 0:
  41.7 50.1 all-gather.4
  94.2 44.0 all-gather.2
where the time goes:
time: 183 us
  local copies, waits for them, and re-layouts  52.8 us (29%)
  waiting for transfers between devices  50.6 us (28%)
  other arithmetic  37.1 us (20%)
  matrix products  22.5 us (12%)
  between operations  15.5 us (8%)
  starting transfers between devices  4.61 us (3%)
    all_gather x1, waiting for transfers between devices, shards(): lax.all_gather(mid_kv, 'seq', axis=1, tiled=True)  26.9 us
    all_gather x1, waiting for transfers between devices, shards(): lax.all_gather(far_kv, 'seq', axis=1, tiled=True)  22.7 us
    reduce_sum x1, other arithmetic, normalize(): row_mean = jnp.mean(mixed_in, axis=1, keepdims=True)  20.1 us
    select_n x4, local copies, waits for them, and re-layouts, scatter_back(): widened = jnp.where(keep[None], flat_out[:, None, :], 0.0)  14.3 us
    dot_general x3, matrix products, attend_single_block(): jnp.einsum('hqk,khd->qhd', weights, value_portion, preferred_element_type...  10.8 us
    unnamed x70, local copies, waits for them, and re-layouts  8.49 us
    slice x2, local copies, waits for them, and re-layouts, shards(): group_kv[0]  6.64 us
    reduce_sum x3, other arithmetic, attend_single_block(): denom_sum = jnp.sum(exp_terms, axis=2)  6.44 us
  transfers between devices with their start and end apart: 4, of which 3 were waited for; matrix products, arithmetic and copies ran while one was open for 22% of the time, Pallas kernels for 0%

commit v1 on v0

--- a/solution.py
+++ b/solution.py
@@ -1,6 +1,10 @@
+import functools
+
 import jax
 import jax.numpy as jnp
 from jax import lax
+from jax.experimental import pallas as pl
+from jax.experimental.pallas import tpu as pltpu
 from jax.sharding import PartitionSpec as P
 
 ATTENTION_HEADS = 16
@@ -183,10 +187,442 @@
     return (attended, encoded)
 
 
+MESH = pl.DeviceIdType.MESH
+LOG2E = 1.4426950408889634
+LANES = 128
+SLOT = 64
+HALO = 2 * GW
+LEAD = 8
+
+
+def head_slots(model_width, head_size):
+    packed = 8 * head_size
+    slotted = 8 * SLOT
+    source = lax.broadcasted_iota(jnp.int32, (packed, slotted), 0)
+    target = lax.broadcasted_iota(jnp.int32, (packed, slotted), 1)
+    inner = target % SLOT
+    match = (inner < head_size) & (source == (target // SLOT) * head_size + inner)
+    return jnp.where(match, 1.0, 0.0).astype(jnp.bfloat16)
+
+
+def head_attention(query, key, value, half, bias, scale):
+    lane = lax.broadcasted_iota(jnp.int32, query.shape, 1)
+    own = jnp.where(lane // SLOT == half, query, jnp.zeros((), query.dtype))
+    scores = lax.dot_general(
+        own, key, (((1,), (1,)), ((), ())), preferred_element_type=jnp.float32
+    )
+    scores = scores * scale + bias
+    top = jnp.max(scores, axis=1, keepdims=True)
+    weights = jnp.exp2(scores - top).astype(jnp.bfloat16)
+    return jnp.dot(weights, value, preferred_element_type=jnp.float32), top
+
+
+def layer_kernel(
+    devices, head_size,
+    count_ref, tiles_ref, conv_w_ref, conv_b_ref, gain_ref, w_qkv_hbm, w_out_hbm,
+    attended_ref, encoded_ref,
+    w_qkv_ref, w_out_ref, halo_lo, halo_hi, ext, mixed, normed, qkv_wide, qkv, bias,
+    near_r, near_m, mid_send, far_send, mid_recv, far_recv, mid_res, far_res,
+    mid_back, far_back, slots_ref, att,
+    w_sem, halo_send_sem, halo_recv_sem, mid_send_sem, mid_recv_sem, far_send_sem, far_recv_sem,
+    mid_bs_sem, mid_br_sem, far_bs_sem, far_br_sem,
+):
+    rows, width = tiles_ref.shape
+    me = lax.axis_index("seq")
+    group = me // MID_RATE
+    place = lax.rem(me, MID_RATE)
+    mid_rows = rows // MID_RATE
+    far_rows = rows // devices
+    tiles_count = ATTENTION_HEADS // 2
+    grid_rows = rows // GW
+    scale = head_size ** (-0.5) * LOG2E
+    count = count_ref[0]
+
+    def weight_copy(i):
+        source, target = ((w_qkv_hbm, w_qkv_ref), (w_out_hbm, w_out_ref))[i]
+        return pltpu.make_async_copy(source, target, w_sem.at[i])
+
+    weight_copy(0).start()
+    weight_copy(1).start()
+
+    barrier = pltpu.get_barrier_semaphore()
+
+    def greet(k, carry):
+        pl.semaphore_signal(
+            barrier, inc=1, device_id={"seq": lax.rem(me + k, devices)}, device_id_type=MESH
+        )
+        return carry
+
+    lax.fori_loop(1, devices, greet, 0)
+
+    base = me * rows
+    row_id = lax.broadcasted_iota(jnp.int32, (rows, 1), 0)
+    valid = base + row_id < count
+
+    def masked_of(block, first):
+        at = first + lax.broadcasted_iota(jnp.int32, (block.shape[0], 1), 0)
+        return jnp.where((at >= 0) & (at < count), block.astype(jnp.float32), 0.0)
+
+    ext[0:LEAD, :] = jnp.zeros((LEAD, width), jnp.float32)
+    ext[LEAD + 2 * HALO + rows :, :] = jnp.zeros((LEAD, width), jnp.float32)
+    ext[LEAD : LEAD + HALO, :] = jnp.zeros((HALO, width), jnp.float32)
+    ext[LEAD + HALO + rows : LEAD + 2 * HALO + rows, :] = jnp.zeros((HALO, width), jnp.float32)
+    ext[LEAD + HALO : LEAD + HALO + rows, :] = masked_of(tiles_ref[...], base)
+
+    pl.semaphore_wait(barrier, devices - 1)
+
+    def up_copy():
+        return pltpu.make_async_remote_copy(
+            src_ref=tiles_ref.at[pl.ds(rows - HALO, HALO), :], dst_ref=halo_lo,
+            send_sem=halo_send_sem.at[0], recv_sem=halo_recv_sem.at[0],
+            device_id={"seq": me + 1}, device_id_type=MESH,
+        )
+
+    def down_copy():
+        return pltpu.make_async_remote_copy(
+            src_ref=tiles_ref.at[pl.ds(0, HALO), :], dst_ref=halo_hi,
+            send_sem=halo_send_sem.at[1], recv_sem=halo_recv_sem.at[1],
+            device_id={"seq": me - 1}, device_id_type=MESH,
+        )
+
+    @pl.when(me < devices - 1)
+    def _():
+        up_copy().start()
+
+    @pl.when(me > 0)
+    def _():
+        down_copy().start()
+
+    slots_ref[...] = head_slots(width, head_size)
+    key_at = lax.broadcasted_iota(jnp.int32, (rows, rows), 1)
+    query_at = lax.broadcasted_iota(jnp.int32, (rows, rows), 0)
+    bias[...] = jnp.where((base + key_at < count) | (query_at == key_at), 0.0, NEG)
+
+    column = lax.broadcasted_iota(jnp.int32, (GW, LANES), 0)
+
+    def conv_rows(r, row_steps, lanes, total):
+        for b in range(-2, 3):
+            part = None
+            for a in row_steps:
+                start = LEAD + HALO + (r + a) * GW + b
+                term = ext[start : start + GW, lanes] * conv_w_ref[
+                    (a + 2) * 5 + b + 2 : (a + 2) * 5 + b + 3, lanes
+                ]
+                part = term if part is None else part + term
+            if b != 0:
+                part = jnp.where((column + b >= 0) & (column + b < GW), part, 0.0)
+            total = total + part
+        return total
+
+    def inner_conv(t, carry):
+        lanes = pl.ds(pl.multiple_of(t * LANES, LANES), LANES)
+        for r in range(grid_rows):
+            here = slice(r * GW, (r + 1) * GW)
+            start = LEAD + HALO + r * GW
+            total = ext[start : start + GW, lanes] + conv_b_ref[:, lanes]
+            steps = [a for a in range(-2, 3) if 0 <= r + a < grid_rows]
+            mixed[here, lanes] = conv_rows(r, steps, lanes, total)
+        return carry
+
+    lax.fori_loop(0, width // LANES, inner_conv, 0)
+
+    @pl.when(me > 0)
+    def _():
+        up_copy().wait_recv()
+        ext[LEAD : LEAD + HALO, :] = masked_of(halo_lo[...], base - HALO)
+
+    @pl.when(me < devices - 1)
+    def _():
+        down_copy().wait_recv()
+        ext[LEAD + HALO + rows : LEAD + 2 * HALO + rows, :] = masked_of(halo_hi[...], base + rows)
+
+    def outer_conv(t, carry):
+        lanes = pl.ds(pl.multiple_of(t * LANES, LANES), LANES)
+        for r in range(grid_rows):
+            here = slice(r * GW, (r + 1) * GW)
+            steps = [a for a in range(-2, 3) if not 0 <= r + a < grid_rows]
+            mixed[here, lanes] = jnp.where(
+                base + r * GW + column < count,
+                conv_rows(r, steps, lanes, mixed[here, lanes]) if steps else mixed[here, lanes],
+                0.0,
+            )
+        return carry
+
+    lax.fori_loop(0, width // LANES, outer_conv, 0)
+
+    def norm_rows(i, carry):
+        here = pl.ds(pl.multiple_of(i * GW, GW), GW)
+        x = mixed[here, :]
+        centred = x - jnp.mean(x, axis=1, keepdims=True)
+        var = jnp.mean(centred * centred, axis=1, keepdims=True)
+        normed[here, :] = (centred * lax.rsqrt(var + EPS) * gain_ref[...]).astype(jnp.bfloat16)
+        return carry
+
+    lax.fori_loop(0, grid_rows, norm_rows, 0)
+
+    lane = lax.broadcasted_iota(jnp.int32, (1, LANES), 1)
+    spare = lane % SLOT >= head_size
+    low = lane < SLOT
+    weight_copy(0).wait()
+    block = 8 * head_size
+    per_block = 8 * SLOT // LANES
+
+    for b in range(3 * width // block):
+        some = jnp.dot(
+            normed[...], w_qkv_ref[:, b * block : (b + 1) * block],
+            preferred_element_type=jnp.float32,
+        ).astype(jnp.bfloat16)
+        spread = jnp.dot(some, slots_ref[...], preferred_element_type=jnp.float32)
+        for i in range(per_block):
+            tile = spread[:, i * LANES : (i + 1) * LANES]
+            if b * block >= 2 * width:
+                tile = jnp.where(spare, 1.0, tile)
+            qkv_wide[b * per_block + i] = tile
+            qkv[b * per_block + i] = tile.astype(jnp.bfloat16)
+
+    for g in range(tiles_count):
+        for c in range(3):
+            from_tile = c * tiles_count + g
+
+            def picked(stride, amount):
+                one = qkv_wide[from_tile, pl.ds((2 * g) % stride, amount, stride=stride), :]
+                two = qkv_wide[from_tile, pl.ds((2 * g + 1) % stride, amount, stride=stride), :]
+                return jnp.where(low, one, two).astype(jnp.bfloat16)
+
+            mid_send[g, c] = picked(MID_RATE, mid_rows)
+            far_send[g, c] = picked(devices, far_rows)
+
+    def mid_at(index):
+        return pl.ds(pl.multiple_of(index * mid_rows, mid_rows), mid_rows)
+
+    def far_at(index):
+        return pl.ds(pl.multiple_of(index * far_rows, far_rows), far_rows)
+
+    def mid_out_copy(k, origin):
+        to = lax.rem(place + k, MID_RATE)
+        return pltpu.make_async_remote_copy(
+            src_ref=mid_send.at[to], dst_ref=mid_recv.at[:, mid_at(origin), :],
+            send_sem=mid_send_sem.at[k], recv_sem=mid_recv_sem.at[k],
+            device_id={"seq": group * MID_RATE + to}, device_id_type=MESH,
+        )
+
+    def far_out_copy(k, origin):
+        to = lax.rem(me + k, devices)
+        return pltpu.make_async_remote_copy(
+            src_ref=far_send.at[to // 2], dst_ref=far_recv.at[:, far_at(origin), :],
+            send_sem=far_send_sem.at[k], recv_sem=far_recv_sem.at[k],
+            device_id={"seq": to}, device_id_type=MESH,
+        )
+
+    def mid_back_copy(k, origin):
+        to = lax.rem(place + k, MID_RATE)
+        return pltpu.make_async_remote_copy(
+            src_ref=mid_res.at[mid_at(to), :], dst_ref=mid_back.at[origin],
+            send_sem=mid_bs_sem.at[k], recv_sem=mid_br_sem.at[k],
+            device_id={"seq": group * MID_RATE + to}, device_id_type=MESH,
+        )
+
+    def far_back_copy(k, origin):
+        to = lax.rem(me + k, devices)
+        return pltpu.make_async_remote_copy(
+            src_ref=far_res.at[far_at(to), :], dst_ref=far_back.at[origin],
+            send_sem=far_bs_sem.at[k], recv_sem=far_br_sem.at[k],
+            device_id={"seq": to}, device_id_type=MESH,
+        )
+
+    def start_all(copy, mine, size):
+        def one(k, carry):
+            copy(k, mine).start()
+            return carry
+
+        lax.fori_loop(1, size, one, 0)
+
+    def receive_all(copy, mine, size):
+        def one(k, carry):
+            copy(k, lax.rem(mine + size - k, size)).wait_recv()
+            return carry
+
+        lax.fori_loop(1, size, one, 0)
+
+    def sent_all(copy, mine, size):
+        def one(k, carry):
+            copy(k, mine).wait_send()
+            return carry
+
+        lax.fori_loop(1, size, one, 0)
+
+    start_all(far_out_copy, me, devices)
+    start_all(mid_out_copy, place, MID_RATE)
+    mid_recv[:, mid_at(place), :] = mid_send[place]
+    far_recv[:, far_at(me), :] = far_send[me // 2]
+
+    def near_pair(g, carry):
+        query, key, value = qkv[g], qkv[tiles_count + g], qkv[2 * tiles_count + g]
+        one, one_top = head_attention(query, key, value, 0, bias[...], scale)
+        two, two_top = head_attention(query, key, value, 1, bias[...], scale)
+        near_r[g] = jnp.where(low, one, two)
+        near_m[g] = jnp.where(low, one_top, two_top)
+        return carry
+
+    before = tiles_count - 2
+    lax.fori_loop(0, before, near_pair, 0)
+
+    def packed(result, top):
+        return jnp.where(lane % SLOT >= SLOT - 8, top, result)
+
+    def level_bias(offset, step, first):
+        at = offset + step * (first + key_at)
+        return jnp.where((at < count) | (query_at == key_at), 0.0, NEG)
+
+    receive_all(mid_out_copy, place, MID_RATE)
+    halves = []
+    for half in range(2):
+        offset = lax.rem(2 * place + half, MID_RATE)
+        halves.append(
+            packed(*head_attention(
+                mid_recv[0], mid_recv[1], mid_recv[2], half,
+                level_bias(offset, MID_RATE, group * rows), scale,
+            ))
+        )
+    mid_res[...] = jnp.where(low, halves[0], halves[1])
+    start_all(mid_back_copy, place, MID_RATE)
+    mid_back[place] = mid_res[mid_at(place), :]
+
+    receive_all(far_out_copy, me, devices)
+    far_res[...] = packed(*head_attention(
+        far_recv[0], far_recv[1], far_recv[2], lax.rem(me, 2),
+        level_bias(me, devices, 0), scale,
+    ))
+    start_all(far_back_copy, me, devices)
+    far_back[me] = far_res[far_at(me), :]
+
+    lax.fori_loop(before, tiles_count, near_pair, 0)
+
+    receive_all(mid_back_copy, place, MID_RATE)
+    receive_all(far_back_copy, me, devices)
+
+    def sum_of(tile):
+        return jnp.where(
+            low, tile[:, head_size : head_size + 1], tile[:, SLOT + head_size : SLOT + head_size + 1]
+        )
+
+    def top_of(tile):
+        return jnp.where(low, tile[:, SLOT - 1 : SLOT], tile[:, 2 * SLOT - 1 : 2 * SLOT])
+
+    def widen(tile, step):
+        return jnp.broadcast_to(
+            tile[:, None, :], (tile.shape[0], step, LANES)
+        ).reshape(rows, LANES)
+
+    def merge_pair(g, carry):
+        head = 2 * g + jnp.where(low, 0, 1)
+        far = jnp.where(low, far_back[2 * g], far_back[2 * g + 1])
+        mid = mid_back[g]
+        mid_on = row_id % MID_RATE == head % MID_RATE
+        far_on = row_id % devices == head % devices
+        near = near_r[g]
+        tops = (
+            near_m[g],
+            jnp.where(mid_on, widen(top_of(mid), MID_RATE), NEG),
+            jnp.where(far_on, widen(top_of(far), devices), NEG),
+        )
+        top = jnp.maximum(jnp.maximum(tops[0], tops[1]), tops[2])
+        factors = [jnp.exp2(one - top) for one in tops]
+        numer = (
+            factors[0] * near
+            + factors[1] * widen(mid, MID_RATE)
+            + factors[2] * widen(far, devices)
+        )
+        denom = (
+            factors[0] * sum_of(near)
+            + factors[1] * widen(sum_of(mid), MID_RATE)
+            + factors[2] * widen(sum_of(far), devices)
+        )
+        att[g] = jnp.where(valid & jnp.logical_not(spare), numer / denom, 0.0).astype(jnp.bfloat16)
+        return carry
+
+    lax.fori_loop(0, tiles_count, merge_pair, 0)
+
+    weight_copy(1).wait()
+    for i in range(width // block):
+        some = jnp.concatenate([att[i * per_block + j] for j in range(per_block)], axis=1)
+        attended_ref[:, i * block : (i + 1) * block] = lax.dot_general(
+            some, slots_ref[...], (((1,), (1,)), ((), ())), preferred_element_type=jnp.float32
+        ).astype(jnp.bfloat16)
+    for i in range(width // block):
+        here = slice(i * block, (i + 1) * block)
+        out = mixed[:, here] + jnp.dot(
+            attended_ref[...], w_out_ref[:, here], preferred_element_type=jnp.float32
+        )
+        encoded_ref[:, here] = jnp.where(valid, out, 0.0).astype(jnp.bfloat16)
+
+    @pl.when(me < devices - 1)
+    def _():
+        up_copy().wait_send()
+
+    @pl.when(me > 0)
+    def _():
+        down_copy().wait_send()
+
+    sent_all(mid_out_copy, place, MID_RATE)
+    sent_all(far_out_copy, me, devices)
+    sent_all(mid_back_copy, place, MID_RATE)
+    sent_all(far_back_copy, me, devices)
+
+
+def fused(tiles, tile_count, conv_weight, conv_bias, ln_gain, w_qkv, w_out):
+    rows, width = tiles.shape
+    devices = lax.axis_size("seq")
+    head_size = width // ATTENTION_HEADS
+    pairs = ATTENTION_HEADS // 2
+    mid_rows, far_rows = rows // MID_RATE, rows // devices
+    bf16, f32 = jnp.bfloat16, jnp.float32
+    vmem = pl.BlockSpec(memory_space=pltpu.VMEM)
+    anyspace = pl.BlockSpec(memory_space=pl.ANY)
+    dma = pltpu.SemaphoreType.DMA
+    return pl.pallas_call(
+        functools.partial(layer_kernel, devices, head_size),
+        out_shape=[jax.ShapeDtypeStruct((rows, width), bf16)] * 2,
+        in_specs=[pl.BlockSpec(memory_space=pltpu.SMEM)] + [vmem] * 4 + [anyspace] * 2,
+        out_specs=[vmem] * 2,
+        scratch_shapes=[
+            pltpu.VMEM(w_qkv.shape, bf16),
+            pltpu.VMEM(w_out.shape, bf16),
+            pltpu.VMEM((HALO, width), bf16),
+            pltpu.VMEM((HALO, width), bf16),
+            pltpu.VMEM((rows + 2 * HALO + 2 * LEAD, width), f32),
+            pltpu.VMEM((rows, width), f32),
+            pltpu.VMEM((rows, width), bf16),
+            pltpu.VMEM((3 * pairs, rows, LANES), f32),
+            pltpu.VMEM((3 * pairs, rows, LANES), bf16),
+            pltpu.VMEM((rows, rows), f32),
+            pltpu.VMEM((pairs, rows, LANES), f32),
+            pltpu.VMEM((pairs, rows, LANES), f32),
+            pltpu.VMEM((pairs, 3, mid_rows, LANES), bf16),
+            pltpu.VMEM((pairs, 3, far_rows, LANES), bf16),
+            pltpu.VMEM((3, rows, LANES), bf16),
+            pltpu.VMEM((3, rows, LANES), bf16),
+            pltpu.VMEM((rows, LANES), f32),
+            pltpu.VMEM((rows, LANES), f32),
+            pltpu.VMEM((pairs, mid_rows, LANES), f32),
+            pltpu.VMEM((ATTENTION_HEADS, far_rows, LANES), f32),
+            pltpu.VMEM((8 * head_size, 8 * SLOT), bf16),
+            pltpu.VMEM((pairs, rows, LANES), bf16),
+            dma((2,)), dma((2,)), dma((2,)),
+            dma((MID_RATE,)), dma((MID_RATE,)), dma((devices,)), dma((devices,)),
+            dma((MID_RATE,)), dma((MID_RATE,)), dma((devices,)), dma((devices,)),
+        ],
+        compiler_params=pltpu.CompilerParams(
+            collective_id=0, has_side_effects=True, vmem_limit_bytes=50 * 1024 * 1024
+        ),
+    )(tile_count, tiles, conv_weight, conv_bias[None], ln_gain[None], w_qkv, w_out)
+
+
 def solution(mesh):
     placed = (P(("slides", "seq"), None), P("slides"), P(), P(), P(), P(), P())
+    body = fused if mesh.shape["seq"] == ATTENTION_HEADS else shards
     return jax.shard_map(
-        shards,
+        body,
         mesh=mesh,
         in_specs=placed,
         out_specs=(P(("slides", "seq"), None), P(("slides", "seq"), None)),

time: 183 us -> 56.6 us (0.31)
  waiting for transfers between devices: 50.6 us -> 0 us
  Pallas kernels: 0 us -> 48.6 us
  local copies, waits for them, and re-layouts: 52.8 us -> 6.44 us
  other arithmetic: 37.1 us -> 0 us
  matrix products: 22.5 us -> 0 us
  between operations: 15.5 us -> 1.29 us
  starting transfers between devices: 4.61 us -> 0 us
    all_gather x2 -> x0, waiting for transfers between devices: 49.6 us -> none  [the longest x1 26.9 us: shards(): lax.all_gather(mid_kv, 'seq', axis=1, tiled=True)]
    pallas_call x0 -> x1, Pallas kernels: none -> 48.6 us  [fused(): pl.pallas_call(functools.partial(layer_kernel, devices, head_size), out_s...]
    reduce_sum x7 -> x0, other arithmetic: 30.5 us -> none  [the longest x1 20.1 us: normalize(): row_mean = jnp.mean(mixed_in, axis=1, keepdims=True)]
    slice x13 -> x0, local copies, waits for them, and re-layouts: 23.9 us -> none  [the longest x2 6.64 us: shards(): group_kv[0]]
    dot_general x8 -> x0, matrix products: 22.5 us -> none  [the longest x3 10.8 us: attend_single_block(): jnp.einsum('hqk,khd->qhd', weights, value_portion, preferred_element_type...]
    select_n x6 -> x0, local copies, waits for them, and re-layouts: 14.6 us -> none  [the longest x4 14.3 us: scatter_back(): widened = jnp.where(keep[None], flat_out[:, None, :], 0.0)]
    ppermute x2 -> x0, starting transfers between devices: 4.35 us -> none  [the longest x1 3.06 us: extended(): lax.ppermute(lax.slice_in_dim(block, block.shape[dim] - width, None, axis...]
    unnamed x70 -> x8, local copies, waits for them, and re-layouts: 8.49 us -> 5.06 us
  transfers between devices with their start and end apart: 4 -> 0, of which waited for: 3 -> 0; matrix products, arithmetic and copies ran while one was open for 22% -> 0% of each run, Pallas kernels for 0% -> 0%
where the time goes in v1:
time: 56.6 us; the launch traced here: 56.3 us
  Pallas kernels  48.6 us (86%)
  local copies, waits for them, and re-layouts  6.44 us (11%)
  between operations  1.29 us (2%)
    pallas_call x1, Pallas kernels, fused(): pl.pallas_call(functools.partial(layer_kernel, devices, head_size), out_s...  48.6 us
    unnamed x8, local copies, waits for them, and re-layouts  5.06 us

profile of v1, /device:TPU:0, one launch (start us, length us, event | category | flops | bytes accessed | tf_op | source)
XLA Modules:
  0.0 56.3 jit_solution(12719039558374252190)
XLA Ops:
  1.3 0.7 %broadcast_in_dim.6.conv_b_ref = f32[1,768]{1,0:T(1,128)S(1)} reshape(f32[768]{0:T(1024)} %param.10) | data formatting | bytes 6144 | tf_op jit(solution)/shard_map/broadcast_in_dim | solution.py:618
  2.0 0.7 %broadcast_in_dim.7.gain_ref = f32[1,768]{1,0:T(1,128)S(1)} reshape(f32[768]{0:T(1024)} %param.11) | data formatting | bytes 6144 | tf_op jit(solution)/shard_map/broadcast_in_dim | solution.py:618
  2.7 0.0 copy-start
  2.7 1.3 %copy-done = bf16[768,768]{1,0:T(8,128)(2,1)S(1)} copy-done((bf16[768,768]{1,0:T(8,128)(2,1)S(1)}, bf16[768,768]{1,0:T(8,128)(2,1)}, u32[]{:S(2)}) %copy-start) | copy-done | bytes 1179672
  3.9 0.0 copy-start.1
  3.9 1.1 %copy-done.1 = bf16[512,768]{1,0:T(8,128)(2,1)S(1)} copy-done((bf16[512,768]{1,0:T(8,128)(2,1)S(1)}, bf16[512,768]{1,0:T(8,128)(2,1)}, u32[]{:S(2)}) %copy-start.1) | copy-done | bytes 786456
  5.1 0.0 copy-start.2
  5.1 0.9 %copy-done.2 = f32[25,768]{1,0:T(8,128)S(1)} copy-done((f32[25,768]{1,0:T(8,128)S(1)}, f32[25,768]{1,0:T(8,128)}, u32[]{:S(2)}) %copy-start.2) | copy-done | bytes 76824
  6.0 48.6 %shard_map.86 = (bf16[512,768]{1,0:T(8,128)(2,1)S(1)}, bf16[512,768]{1,0:T(8,128)(2,1)S(1)}) custom-call(s32[1]{0:T(128)S(6)} %copy.11.count_ref, bf16[512,768]{1,0:T(8,128)(2,1)S(1)} %copy-done.1, f32[25,768]{1,0:T(8,128)S(1)} %copy-done.2, f32[1,768]{1,0:T(1,128)S(1)} %broadcast_in_dim.6.conv_b_ref, f32[1,768]{1,0:T(1,128)S(1)} %broadcast_in_dim.7.gain_ref, ...), custom_call_target="tpu_custom_call" | custom-call | tf_op jit(solution)/shard_map/pallas_call | solution.py:583
  54.5 0.9 %copy.12 = bf16[512,768]{1,0:T(8,128)(2,1)} copy(bf16[512,768]{1,0:T(8,128)(2,1)S(1)} %get-tuple-element.4) | data formatting | bytes 1572864
  55.4 0.9 %copy.13 = bf16[512,768]{1,0:T(8,128)(2,1)} copy(bf16[512,768]{1,0:T(8,128)(2,1)S(1)} %get-tuple-element.5) | data formatting | bytes 1572864
Async XLA Ops:
  2.7 1.3 %copy-start = (bf16[768,768]{1,0:T(8,128)(2,1)S(1)}, bf16[768,768]{1,0:T(8,128)(2,1)}, u32[]{:S(2)}) copy-start(bf16[768,768]{1,0:T(8,128)(2,1)} %w_out_hbm.1) | copy-start | bytes 3538948
  3.9 1.1 %copy-start.1 = (bf16[512,768]{1,0:T(8,128)(2,1)S(1)}, bf16[512,768]{1,0:T(8,128)(2,1)}, u32[]{:S(2)}) copy-start(bf16[512,768]{1,0:T(8,128)(2,1)} %tiles_ref.1) | copy-start | bytes 2359300
  5.1 0.9 %copy-start.2 = (f32[25,768]{1,0:T(8,128)S(1)}, f32[25,768]{1,0:T(8,128)}, u32[]{:S(2)}) copy-start(f32[25,768]{1,0:T(8,128)} %conv_w_ref.1) | copy-start | bytes 230404

commit v2 on v1

--- a/solution.py
+++ b/solution.py
@@ -219,9 +219,9 @@
 
 def layer_kernel(
     devices, head_size,
-    count_ref, tiles_ref, conv_w_ref, conv_b_ref, gain_ref, w_qkv_hbm, w_out_hbm,
+    count_ref, tiles_hbm, conv_w_hbm, conv_b_hbm, gain_hbm, w_qkv_hbm, w_out_hbm,
     attended_ref, encoded_ref,
-    w_qkv_ref, w_out_ref, halo_lo, halo_hi, ext, mixed, normed, qkv_wide, qkv, bias,
+    tiles_ref, conv_w_ref, conv_b_ref, gain_ref, w_qkv_ref, w_out_ref, halo_lo, halo_hi, ext, mixed, normed, qkv_wide, qkv, bias,
     near_r, near_m, mid_send, far_send, mid_recv, far_recv, mid_res, far_res,
     mid_back, far_back, slots_ref, att,
     w_sem, halo_send_sem, halo_recv_sem, mid_send_sem, mid_recv_sem, far_send_sem, far_recv_sem,
@@ -239,11 +239,14 @@
     count = count_ref[0]
 
     def weight_copy(i):
-        source, target = ((w_qkv_hbm, w_qkv_ref), (w_out_hbm, w_out_ref))[i]
+        source, target = (
+            (w_qkv_hbm, w_qkv_ref), (w_out_hbm, w_out_ref), (tiles_hbm, tiles_ref),
+            (conv_w_hbm, conv_w_ref), (conv_b_hbm, conv_b_ref), (gain_hbm, gain_ref),
+        )[i]
         return pltpu.make_async_copy(source, target, w_sem.at[i])
 
-    weight_copy(0).start()
-    weight_copy(1).start()
+    for i in (2, 3, 4, 5, 0, 1):
+        weight_copy(i).start()
 
     barrier = pltpu.get_barrier_semaphore()
 
@@ -267,20 +270,18 @@
     ext[LEAD + 2 * HALO + rows :, :] = jnp.zeros((LEAD, width), jnp.float32)
     ext[LEAD : LEAD + HALO, :] = jnp.zeros((HALO, width), jnp.float32)
     ext[LEAD + HALO + rows : LEAD + 2 * HALO + rows, :] = jnp.zeros((HALO, width), jnp.float32)
-    ext[LEAD + HALO : LEAD + HALO + rows, :] = masked_of(tiles_ref[...], base)
-
     pl.semaphore_wait(barrier, devices - 1)
 
     def up_copy():
         return pltpu.make_async_remote_copy(
-            src_ref=tiles_ref.at[pl.ds(rows - HALO, HALO), :], dst_ref=halo_lo,
+            src_ref=tiles_hbm.at[pl.ds(rows - HALO, HALO), :], dst_ref=halo_lo,
             send_sem=halo_send_sem.at[0], recv_sem=halo_recv_sem.at[0],
             device_id={"seq": me + 1}, device_id_type=MESH,
         )
 
     def down_copy():
         return pltpu.make_async_remote_copy(
-            src_ref=tiles_ref.at[pl.ds(0, HALO), :], dst_ref=halo_hi,
+            src_ref=tiles_hbm.at[pl.ds(0, HALO), :], dst_ref=halo_hi,
             send_sem=halo_send_sem.at[1], recv_sem=halo_recv_sem.at[1],
             device_id={"seq": me - 1}, device_id_type=MESH,
         )
@@ -293,6 +294,9 @@
     def _():
         down_copy().start()
 
+    for i in (2, 3, 4, 5):
+        weight_copy(i).wait()
+    ext[LEAD + HALO : LEAD + HALO + rows, :] = masked_of(tiles_ref[...], base)
     slots_ref[...] = head_slots(width, head_size)
     key_at = lax.broadcasted_iota(jnp.int32, (rows, rows), 1)
     query_at = lax.broadcasted_iota(jnp.int32, (rows, rows), 0)
@@ -319,7 +323,7 @@
         for r in range(grid_rows):
             here = slice(r * GW, (r + 1) * GW)
             start = LEAD + HALO + r * GW
-            total = ext[start : start + GW, lanes] + conv_b_ref[:, lanes]
+            total = ext[start : start + GW, lanes] + conv_b_ref[lanes][None]
             steps = [a for a in range(-2, 3) if 0 <= r + a < grid_rows]
             mixed[here, lanes] = conv_rows(r, steps, lanes, total)
         return carry
@@ -355,7 +359,7 @@
         x = mixed[here, :]
         centred = x - jnp.mean(x, axis=1, keepdims=True)
         var = jnp.mean(centred * centred, axis=1, keepdims=True)
-        normed[here, :] = (centred * lax.rsqrt(var + EPS) * gain_ref[...]).astype(jnp.bfloat16)
+        normed[here, :] = (centred * lax.rsqrt(var + EPS) * gain_ref[...][None]).astype(jnp.bfloat16)
         return carry
 
     lax.fori_loop(0, grid_rows, norm_rows, 0)
@@ -380,23 +384,34 @@
             qkv_wide[b * per_block + i] = tile
             qkv[b * per_block + i] = tile.astype(jnp.bfloat16)
 
+    fold = far_rows // 2
+
+    def swapped(x):
+        return pltpu.roll(x, SLOT, x.ndim - 1)
+
     for g in range(tiles_count):
         for c in range(3):
             from_tile = c * tiles_count + g
 
-            def picked(stride, amount):
-                one = qkv_wide[from_tile, pl.ds((2 * g) % stride, amount, stride=stride), :]
-                two = qkv_wide[from_tile, pl.ds((2 * g + 1) % stride, amount, stride=stride), :]
-                return jnp.where(low, one, two).astype(jnp.bfloat16)
-
-            mid_send[g, c] = picked(MID_RATE, mid_rows)
-            far_send[g, c] = picked(devices, far_rows)
+            one = qkv_wide[from_tile, pl.ds((2 * g) % MID_RATE, mid_rows, stride=MID_RATE), :]
+            two = qkv_wide[from_tile, pl.ds((2 * g + 1) % MID_RATE, mid_rows, stride=MID_RATE), :]
+            mid_send[g, c] = jnp.where(low, one, two).astype(jnp.bfloat16)
+        for half in range(2):
+            query, key, value = (
+                qkv_wide[c * tiles_count + g, pl.ds(2 * g + half, far_rows, stride=devices), :]
+                for c in range(3)
+            )
+            if half == 0:
+                key, last = swapped(key), swapped(value[fold:])
+                first = value[:fold]
+            else:
+                query, first = swapped(query), swapped(value[:fold])
+                last = value[fold:]
+            far_send[2 * g + half, :far_rows] = jnp.where(low, query, key).astype(jnp.bfloat16)
+            far_send[2 * g + half, far_rows:] = jnp.where(low, first, last).astype(jnp.bfloat16)
 
     def mid_at(index):
         return pl.ds(pl.multiple_of(index * mid_rows, mid_rows), mid_rows)
-
-    def far_at(index):
-        return pl.ds(pl.multiple_of(index * far_rows, far_rows), far_rows)
 
     def mid_out_copy(k, origin):
         to = lax.rem(place + k, MID_RATE)
@@ -409,7 +424,7 @@
     def far_out_copy(k, origin):
         to = lax.rem(me + k, devices)
         return pltpu.make_async_remote_copy(
-            src_ref=far_send.at[to // 2], dst_ref=far_recv.at[:, far_at(origin), :],
+            src_ref=far_send.at[to], dst_ref=far_recv.at[origin],
             send_sem=far_send_sem.at[k], recv_sem=far_recv_sem.at[k],
             device_id={"seq": to}, device_id_type=MESH,
         )
@@ -425,7 +440,7 @@
     def far_back_copy(k, origin):
         to = lax.rem(me + k, devices)
         return pltpu.make_async_remote_copy(
-            src_ref=far_res.at[far_at(to), :], dst_ref=far_back.at[origin],
+            src_ref=far_res.at[to], dst_ref=far_back.at[origin],
             send_sem=far_bs_sem.at[k], recv_sem=far_br_sem.at[k],
             device_id={"seq": to}, device_id_type=MESH,
         )
@@ -454,7 +469,7 @@
     start_all(far_out_copy, me, devices)
     start_all(mid_out_copy, place, MID_RATE)
     mid_recv[:, mid_at(place), :] = mid_send[place]
-    far_recv[:, far_at(me), :] = far_send[me // 2]
+    far_recv[me] = far_send[me]
 
     def near_pair(g, carry):
         query, key, value = qkv[g], qkv[tiles_count + g], qkv[2 * tiles_count + g]
@@ -464,37 +479,54 @@
         near_m[g] = jnp.where(low, one_top, two_top)
         return carry
 
-    before = tiles_count - 2
+    before = tiles_count - 3
     lax.fori_loop(0, before, near_pair, 0)
 
-    def packed(result, top):
-        return jnp.where(lane % SLOT >= SLOT - 8, top, result)
+    inner = lane % SLOT
+    piece = (SLOT - head_size) // 3
+    places = (head_size, head_size + piece, head_size + 2 * piece)
+
+    def packed(result, top, denom):
+        total = top + jnp.log(denom) * LOG2E
+        first = total.astype(jnp.bfloat16).astype(jnp.float32)
+        second = (total - first).astype(jnp.bfloat16).astype(jnp.float32)
+        third = total - first - second
+        sums = jnp.where(inner < places[1], first, jnp.where(inner < places[2], second, third))
+        return jnp.where(spare, sums, result / denom)
 
     def level_bias(offset, step, first):
         at = offset + step * (first + key_at)
         return jnp.where((at < count) | (query_at == key_at), 0.0, NEG)
+
+    receive_all(far_out_copy, me, devices)
+    both = far_recv[:, :far_rows, :].astype(jnp.float32).reshape(rows, LANES)
+    folded = far_recv[:, far_rows:, :].astype(jnp.float32)
+    far_value = jnp.concatenate([folded, swapped(folded)], axis=1).reshape(rows, LANES)
+    result, top = head_attention(
+        both.astype(jnp.bfloat16), swapped(both).astype(jnp.bfloat16),
+        far_value.astype(jnp.bfloat16), 0, level_bias(me, devices, 0), scale,
+    )
+    result = packed(result, top, result[:, head_size : head_size + 1])
+    result = result.reshape(devices, far_rows, LANES)
+    far_res[...] = jnp.where(low[None], result[:, :fold], swapped(result[:, fold:])).astype(
+        jnp.bfloat16
+    )
+    start_all(far_back_copy, me, devices)
+    far_back[me] = far_res[me]
 
     receive_all(mid_out_copy, place, MID_RATE)
     halves = []
     for half in range(2):
         offset = lax.rem(2 * place + half, MID_RATE)
-        halves.append(
-            packed(*head_attention(
-                mid_recv[0], mid_recv[1], mid_recv[2], half,
-                level_bias(offset, MID_RATE, group * rows), scale,
-            ))
-        )
-    mid_res[...] = jnp.where(low, halves[0], halves[1])
+        result, top = head_attention(
+            mid_recv[0], mid_recv[1], mid_recv[2], half,
+            level_bias(offset, MID_RATE, group * rows), scale,
+        )
+        at = half * SLOT + head_size
+        halves.append(packed(result, top, result[:, at : at + 1]))
+    mid_res[...] = jnp.where(low, halves[0], halves[1]).astype(jnp.bfloat16)
     start_all(mid_back_copy, place, MID_RATE)
     mid_back[place] = mid_res[mid_at(place), :]
-
-    receive_all(far_out_copy, me, devices)
-    far_res[...] = packed(*head_attention(
-        far_recv[0], far_recv[1], far_recv[2], lax.rem(me, 2),
-        level_bias(me, devices, 0), scale,
-    ))
-    start_all(far_back_copy, me, devices)
-    far_back[me] = far_res[far_at(me), :]
 
     lax.fori_loop(before, tiles_count, near_pair, 0)
 
@@ -506,8 +538,11 @@
             low, tile[:, head_size : head_size + 1], tile[:, SLOT + head_size : SLOT + head_size + 1]
         )
 
-    def top_of(tile):
-        return jnp.where(low, tile[:, SLOT - 1 : SLOT], tile[:, 2 * SLOT - 1 : 2 * SLOT])
+    def log_of(tile):
+        def at(half):
+            return sum(tile[:, half * SLOT + i : half * SLOT + i + 1] for i in places)
+
+        return jnp.where(low, at(0), at(1))
 
     def widen(tile, step):
         return jnp.broadcast_to(
@@ -516,15 +551,21 @@
 
     def merge_pair(g, carry):
         head = 2 * g + jnp.where(low, 0, 1)
-        far = jnp.where(low, far_back[2 * g], far_back[2 * g + 1])
-        mid = mid_back[g]
+        one = far_back[2 * g].astype(jnp.float32)
+        two = far_back[2 * g + 1].astype(jnp.float32)
+        far = jnp.where(
+            low,
+            jnp.concatenate([one, swapped(one)], axis=0),
+            jnp.concatenate([swapped(two), two], axis=0),
+        )
+        mid = mid_back[g].astype(jnp.float32)
         mid_on = row_id % MID_RATE == head % MID_RATE
         far_on = row_id % devices == head % devices
         near = near_r[g]
         tops = (
             near_m[g],
-            jnp.where(mid_on, widen(top_of(mid), MID_RATE), NEG),
-            jnp.where(far_on, widen(top_of(far), devices), NEG),
+            jnp.where(mid_on, widen(log_of(mid), MID_RATE), NEG),
+            jnp.where(far_on, widen(log_of(far), devices), NEG),
         )
         top = jnp.maximum(jnp.maximum(tops[0], tops[1]), tops[2])
         factors = [jnp.exp2(one - top) for one in tops]
@@ -533,11 +574,7 @@
             + factors[1] * widen(mid, MID_RATE)
             + factors[2] * widen(far, devices)
         )
-        denom = (
-            factors[0] * sum_of(near)
-            + factors[1] * widen(sum_of(mid), MID_RATE)
-            + factors[2] * widen(sum_of(far), devices)
-        )
+        denom = factors[0] * sum_of(near) + factors[1] + factors[2]
         att[g] = jnp.where(valid & jnp.logical_not(spare), numer / denom, 0.0).astype(jnp.bfloat16)
         return carry
 
@@ -583,9 +620,13 @@
     return pl.pallas_call(
         functools.partial(layer_kernel, devices, head_size),
         out_shape=[jax.ShapeDtypeStruct((rows, width), bf16)] * 2,
-        in_specs=[pl.BlockSpec(memory_space=pltpu.SMEM)] + [vmem] * 4 + [anyspace] * 2,
+        in_specs=[pl.BlockSpec(memory_space=pltpu.SMEM)] + [anyspace] * 6,
         out_specs=[vmem] * 2,
         scratch_shapes=[
+            pltpu.VMEM((rows, width), bf16),
+            pltpu.VMEM(conv_weight.shape, f32),
+            pltpu.VMEM((width,), f32),
+            pltpu.VMEM((width,), f32),
             pltpu.VMEM(w_qkv.shape, bf16),
             pltpu.VMEM(w_out.shape, bf16),
             pltpu.VMEM((HALO, width), bf16),
@@ -599,23 +640,23 @@
             pltpu.VMEM((pairs, rows, LANES), f32),
             pltpu.VMEM((pairs, rows, LANES), f32),
             pltpu.VMEM((pairs, 3, mid_rows, LANES), bf16),
-            pltpu.VMEM((pairs, 3, far_rows, LANES), bf16),
+            pltpu.VMEM((devices, 3 * far_rows // 2, LANES), bf16),
             pltpu.VMEM((3, rows, LANES), bf16),
-            pltpu.VMEM((3, rows, LANES), bf16),
-            pltpu.VMEM((rows, LANES), f32),
-            pltpu.VMEM((rows, LANES), f32),
-            pltpu.VMEM((pairs, mid_rows, LANES), f32),
-            pltpu.VMEM((ATTENTION_HEADS, far_rows, LANES), f32),
+            pltpu.VMEM((devices, 3 * far_rows // 2, LANES), bf16),
+            pltpu.VMEM((rows, LANES), bf16),
+            pltpu.VMEM((devices, far_rows // 2, LANES), bf16),
+            pltpu.VMEM((pairs, mid_rows, LANES), bf16),
+            pltpu.VMEM((devices, far_rows // 2, LANES), bf16),
             pltpu.VMEM((8 * head_size, 8 * SLOT), bf16),
             pltpu.VMEM((pairs, rows, LANES), bf16),
-            dma((2,)), dma((2,)), dma((2,)),
+            dma((6,)), dma((2,)), dma((2,)),
             dma((MID_RATE,)), dma((MID_RATE,)), dma((devices,)), dma((devices,)),
             dma((MID_RATE,)), dma((MID_RATE,)), dma((devices,)), dma((devices,)),
         ],
         compiler_params=pltpu.CompilerParams(
             collective_id=0, has_side_effects=True, vmem_limit_bytes=50 * 1024 * 1024
         ),
-    )(tile_count, tiles, conv_weight, conv_bias[None], ln_gain[None], w_qkv, w_out)
+    )(tile_count, tiles, conv_weight, conv_bias, ln_gain, w_qkv, w_out)
 
 
 def solution(mesh):

time: 56.6 us -> 50.9 us (0.90)
  Pallas kernels: 48.6 us -> 42.9 us
    pallas_call x1, Pallas kernels: 48.6 us -> 42.9 us  [fused(): pl.pallas_call(functools.partial(layer_kernel, devices, head_size), out_s...]
    broadcast_in_dim x2 -> x0, local copies, waits for them, and re-layouts: 1.38 us -> none  [the longest x1 0.69 us: fused(): conv_bias[None]]
    unnamed x8 -> x12, local copies, waits for them, and re-layouts: 5.06 us -> 6.42 us
where the time goes in v2:
time: 50.9 us; the launch traced here: 50.6 us
  Pallas kernels  42.9 us (84%)
  local copies, waits for them, and re-layouts  6.42 us (13%)
  between operations  1.3 us (3%)
    pallas_call x1, Pallas kernels, fused(): pl.pallas_call(functools.partial(layer_kernel, devices, head_size), out_s...  42.9 us
    unnamed x12, local copies, waits for them, and re-layouts  6.42 us

profile of v2, /device:TPU:0, one launch (start us, length us, event | category | flops | bytes accessed | tf_op | source)
XLA Modules:
  0.0 50.6 jit_solution(10826993955716215378)
XLA Ops:
  1.3 0.0 copy-start
  1.3 1.3 %copy-done = bf16[768,768]{1,0:T(8,128)(2,1)S(1)} copy-done((bf16[768,768]{1,0:T(8,128)(2,1)S(1)}, bf16[768,768]{1,0:T(8,128)(2,1)}, u32[]{:S(2)}) %copy-start) | copy-done | bytes 1179672
  2.5 0.0 copy-start.1
  2.6 1.1 %copy-done.1 = bf16[512,768]{1,0:T(8,128)(2,1)S(1)} copy-done((bf16[512,768]{1,0:T(8,128)(2,1)S(1)}, bf16[512,768]{1,0:T(8,128)(2,1)}, u32[]{:S(2)}) %copy-start.1) | copy-done | bytes 786456
  3.7 0.0 copy-start.2
  3.7 0.9 %copy-done.2 = f32[25,768]{1,0:T(8,128)S(1)} copy-done((f32[25,768]{1,0:T(8,128)S(1)}, f32[25,768]{1,0:T(8,128)}, u32[]{:S(2)}) %copy-start.2) | copy-done | bytes 76824
  4.6 0.0 copy-start.3
  4.6 0.7 %copy-done.3 = f32[768]{0:T(1024)S(1)} copy-done((f32[768]{0:T(1024)S(1)}, f32[768]{0:T(1024)}, u32[]{:S(2)}) %copy-start.3) | copy-done | bytes 3096
  5.3 0.0 copy-start.4
  5.3 0.7 %copy-done.4 = f32[768]{0:T(1024)S(1)} copy-done((f32[768]{0:T(1024)S(1)}, f32[768]{0:T(1024)}, u32[]{:S(2)}) %copy-start.4) | copy-done | bytes 3096
  6.0 42.9 %shard_map.86 = (bf16[512,768]{1,0:T(8,128)(2,1)S(1)}, bf16[512,768]{1,0:T(8,128)(2,1)S(1)}) custom-call(s32[1]{0:T(128)S(6)} %copy.11.count_ref, bf16[512,768]{1,0:T(8,128)(2,1)S(1)} %copy-done.1, f32[25,768]{1,0:T(8,128)S(1)} %copy-done.2, f32[768]{0:T(1024)S(1)} %copy-done.3, f32[768]{0:T(1024)S(1)} %copy-done.4, bf16[768,2304]{1,0:T(8,128)(2,1)} %w_qkv_hbm.1, ...), custom_call_target="tpu_custom_call" | custom-call | tf_op jit(solution)/shard_map/pallas_call | solution.py:620
  48.8 0.9 %copy.12 = bf16[512,768]{1,0:T(8,128)(2,1)} copy(bf16[512,768]{1,0:T(8,128)(2,1)S(1)} %get-tuple-element.4) | data formatting | bytes 1572864
  49.7 0.9 %copy.13 = bf16[512,768]{1,0:T(8,128)(2,1)} copy(bf16[512,768]{1,0:T(8,128)(2,1)S(1)} %get-tuple-element.5) | data formatting | bytes 1572864
Async XLA Ops:
  1.3 1.3 %copy-start = (bf16[768,768]{1,0:T(8,128)(2,1)S(1)}, bf16[768,768]{1,0:T(8,128)(2,1)}, u32[]{:S(2)}) copy-start(bf16[768,768]{1,0:T(8,128)(2,1)} %w_out_hbm.1) | copy-start | bytes 3538948
  2.5 1.1 %copy-start.1 = (bf16[512,768]{1,0:T(8,128)(2,1)S(1)}, bf16[512,768]{1,0:T(8,128)(2,1)}, u32[]{:S(2)}) copy-start(bf16[512,768]{1,0:T(8,128)(2,1)} %tiles_hbm.1) | copy-start | bytes 2359300
  3.7 0.9 %copy-start.2 = (f32[25,768]{1,0:T(8,128)S(1)}, f32[25,768]{1,0:T(8,128)}, u32[]{:S(2)}) copy-start(f32[25,768]{1,0:T(8,128)} %conv_w_hbm.1) | copy-start | bytes 230404
  4.6 0.7 %copy-start.3 = (f32[768]{0:T(1024)S(1)}, f32[768]{0:T(1024)}, u32[]{:S(2)}) copy-start(f32[768]{0:T(1024)} %conv_b_hbm.1) | copy-start | bytes 9220
  5.3 0.7 %copy-start.4 = (f32[768]{0:T(1024)S(1)}, f32[768]{0:T(1024)}, u32[]{:S(2)}) copy-start(f32[768]{0:T(1024)} %gain_hbm.1) | copy-start | bytes 9220

commit v3 on v2

--- a/solution.py
+++ b/solution.py
@@ -615,12 +615,12 @@
     mid_rows, far_rows = rows // MID_RATE, rows // devices
     bf16, f32 = jnp.bfloat16, jnp.float32
     vmem = pl.BlockSpec(memory_space=pltpu.VMEM)
-    anyspace = pl.BlockSpec(memory_space=pl.ANY)
+    hbm = pl.BlockSpec(memory_space=pltpu.HBM)
     dma = pltpu.SemaphoreType.DMA
     return pl.pallas_call(
         functools.partial(layer_kernel, devices, head_size),
         out_shape=[jax.ShapeDtypeStruct((rows, width), bf16)] * 2,
-        in_specs=[pl.BlockSpec(memory_space=pltpu.SMEM)] + [anyspace] * 6,
+        in_specs=[pl.BlockSpec(memory_space=pltpu.SMEM)] + [hbm] * 6,
         out_specs=[vmem] * 2,
         scratch_shapes=[
             pltpu.VMEM((rows, width), bf16),
@@ -654,7 +654,7 @@
             dma((MID_RATE,)), dma((MID_RATE,)), dma((devices,)), dma((devices,)),
         ],
         compiler_params=pltpu.CompilerParams(
-            collective_id=0, has_side_effects=True, vmem_limit_bytes=50 * 1024 * 1024
+            collective_id=0, has_side_effects=True, vmem_limit_bytes=60 * 1024 * 1024
         ),
     )(tile_count, tiles, conv_weight, conv_bias, ln_gain, w_qkv, w_out)
 

time: 50.9 us -> 49.5 us (0.972)
  local copies, waits for them, and re-layouts: 6.42 us -> 4.13 us
  Pallas kernels: 42.9 us -> 43.8 us
    unnamed x12 -> x2, local copies, waits for them, and re-layouts: 6.42 us -> 4.13 us
    pallas_call x1, Pallas kernels: 42.9 us -> 43.8 us  [fused(): pl.pallas_call(functools.partial(layer_kernel, devices, head_size), out_s...]
where the time goes in v3:
time: 49.5 us; the launch traced here: 49.2 us
  Pallas kernels  43.8 us (88%)
  local copies, waits for them, and re-layouts  4.13 us (8%)
  between operations  1.29 us (3%)
    pallas_call x1, Pallas kernels, fused(): pl.pallas_call(functools.partial(layer_kernel, devices, head_size), out_s...  43.8 us
    unnamed x2, local copies, waits for them, and re-layouts  4.13 us

profile of v3, /device:TPU:0, one launch (start us, length us, event | category | flops | bytes accessed | tf_op | source)
XLA Modules:
  0.0 49.2 jit_solution(11067338722131972122)
XLA Ops:
  1.3 43.8 %shard_map.86 = (bf16[512,768]{1,0:T(8,128)(2,1)}, bf16[512,768]{1,0:T(8,128)(2,1)}) custom-call(s32[1]{0:T(128)S(6)} %copy.11.count_ref, bf16[512,768]{1,0:T(8,128)(2,1)} %tiles_hbm.1, f32[25,768]{1,0:T(8,128)} %conv_w_hbm.1, f32[768]{0:T(1024)} %conv_b_hbm.1, f32[768]{0:T(1024)} %gain_hbm.1, bf16[768,2304]{1,0:T(8,128)(2,1)} %w_qkv_hbm.1, ...), custom_call_target="tpu_custom_call" | custom-call | tf_op jit(solution)/shard_map/pallas_call | solution.py:620
  45.1 2.1 %copy.12 = bf16[512,768]{1,0:T(8,128)(2,1)} copy(bf16[512,768]{1,0:T(8,128)(2,1)} %get-tuple-element.4) | data formatting | bytes 1572864
  47.2 2.1 %copy.13 = bf16[512,768]{1,0:T(8,128)(2,1)} copy(bf16[512,768]{1,0:T(8,128)(2,1)} %get-tuple-element.5) | data formatting | bytes 1572864
